TPU v7x, 128 devices: a whole 4x4x4 slice. The times are simulated.
128 devices in a mesh: row: 8 (over y, core), col: 16 (over x, z).
Axes of the slice: x: 4, y: 4, z: 4, core: 2. Of those that a mesh axis runs over, the one named last changes fastest.
Arguments:
- kernels: bfloat16 [6, 16384, 12288], P(None, 'col', 'row'), may hold values from -0.0234375 to 0.0234375
- history: bfloat16 [6, 12288, 256], P(None, ('row', 'col')), may hold values from -6 to 6
- incident: float32 [128, 128, 256], P(('row', 'col')), may hold values from -6 to 6
- owner: int32 [128], replicated, may hold values from 0 to 7, as said below
- tile_pairs: int32 [1536, 2], P(('row', 'col')), may hold values from 0 to 127, as said below
- tile_values: bfloat16 [1536, 128, 128], P(('row', 'col')), may hold values from -0.109375 to 0.109375
- tile_counts: int32 [128], P(('row', 'col')), may hold values from 1 to 12, as said below
Outputs:
- density: float32 [128, 128, 256], P(('row', 'col'))
Inputs may be any that keep to these rules, and one draw needn't show every extreme that they name: `owner`: within each block of 8 consecutive clusters starting at a multiple of 8, the owners are all different. tile_pairs[t, 0] is the cluster whose slot is t // 12; for a target cluster k the sources of its slot are distinct clusters whose block (cluster // 8) is k // 8 - 1, k // 8 or k // 8 + 1, modulo 16. `tile_counts`: some device has all 12 slots live.
All inputs are finite; a program needn't handle non-finite values.
Results may differ from a plain program's by a relative error of at most 0.0012.
Values may be sent and summed in bfloat16 or wider, within the bound.
A program may use at most 128 MiB of HBM per device.

v0:
```python
import jax
import jax.numpy as jnp
from jax import lax
from jax.sharding import PartitionSpec as P

SWEEPS = 3


damping = 0.7


def per_device(kernels, history, incident, owner, tile_pairs, tile_values, tile_counts):
    row_count = lax.axis_size("row")
    col_count = lax.axis_size("col")
    columns = history.shape[2]
    cluster = incident.shape[1]
    retarded = lax.dot_general(
        kernels,
        lax.all_gather(history, "col", axis=1, tiled=True),
        (((0, 2), (0, 1)), ((), ())),
        preferred_element_type=jnp.float32,
    )
    col_index = lax.axis_index("col")
    row_index = lax.axis_index("row")
    block_owner = lax.dynamic_slice_in_dim(owner, col_index * row_count, row_count)
    positions = jnp.arange(row_count, dtype=jnp.int32)
    blocks = retarded.reshape(row_count, cluster, columns)
    block_sum = lax.psum_scatter(blocks, "row", scatter_dimension=0, tiled=True)
    everyone = lax.all_gather(block_sum, "row", axis=0, tiled=True)
    chosen = jnp.sum(jnp.where(block_owner == row_index, positions, 0))
    owned_sum = lax.dynamic_index_in_dim(everyone, chosen, 0, keepdims=False)
    driven = incident[0] - owned_sum
    sources = tile_pairs[:, 1]
    clusters = jnp.arange(owner.shape[0], dtype=jnp.int32)
    src_owner = jnp.sum(jnp.where(sources[:, None] == clusters[None, :], owner[None, :], 0), axis=1)
    src_slot = src_owner * col_count + sources // row_count
    active = jnp.arange(tile_values.shape[0], dtype=jnp.int32) < tile_counts[0]
    density = driven
    for sweep_step in range(SWEEPS):
        rounded = density.astype(jnp.bfloat16)
        gathered = lax.all_gather(rounded, ("row", "col"), axis=0, tiled=True)
        gathered = gathered.reshape(-1, cluster, columns)
        picked = jnp.take(gathered, src_slot, axis=0)
        picked = jnp.where(active[:, None, None], picked, jnp.zeros((), jnp.bfloat16))
        near_term = lax.dot_general(
            tile_values, picked, (((0, 2), (0, 1)), ((), ())), preferred_element_type=jnp.float32
        )
        density = density + damping * (driven - density - near_term)
    return density[None]


def solution(mesh):
    in_specs = (
        P(None, "col", "row"),
        P(None, ("row", "col"), None),
        P(("row", "col"), None, None),
        P(),
        P(("row", "col"), None),
        P(("row", "col"), None, None),
        P(("row", "col")),
    )
    out_specs = P(("row", "col"), None, None)
    return jax.shard_map(
        per_device, mesh=mesh, in_specs=in_specs, out_specs=out_specs, check_vma=False
    )
```

profile of v0, /device:TPU:1, one launch (start us, length us, event | category | flops | bytes accessed | tf_op | source)
XLA Modules:
  0.0 431.1 jit_solution(3455106230018565582)
XLA Ops:
  6.5 0.7 all-gather.6.cloned.1.call-update
  7.3 0.0 reduce-scatter.2.cloned.1.call-start
  7.3 59.5 %all-gather.6.cloned.1.call-done = bf16[6,1536,256]{2,1,0:T(8,128)(2,1)} async-done(((bf16[6,96,256]{2,1,0:T(8,128)(2,1)}), bf16[6,1536,256]{2,1,0:T(8,128)(2,1)}) %all-gather.6.cloned.1.call-update) | async-done | bytes 4718608 | tf_op jit(solution)/shard_map/all_gather | solution.py:19
  66.8 11.1 %fusion.31 = f32[1024,256,1]{1,0,2:T(8,128)} fusion(bf16[6,1024,1536]{2,1,0:T(8,128)(2,1)} %param.9, bf16[6,1536,256]{2,1,0:T(8,128)(2,1)} %all-gather.6.cloned.1.call-done), kind=kOutput, calls=%fused_computation.57 | convolution fusion | flops 4831838208 | bytes 24641536 | tf_op jit(solution)/shard_map/dot_general | solution.py:17
  78.0 0.0 reduce-scatter.2.cloned.1.call-update
  78.0 0.0 all-gather.8.cloned.1.call-start
  78.1 28.8 %reduce-scatter.2.cloned.1.call-done = f32[1,128,256]{2,1,0:T(8,128)} async-done(((f32[8,128,256]{2,1,0:T(8,128)}), f32[1,128,256]{2,1,0:T(8,128)}) %reduce-scatter.2.cloned.1.call-update) | async-done | bytes 131088 | tf_op jit(solution)/shard_map/reduce_scatter | solution.py:28
  106.8 0.0 all-gather.8.cloned.1.call-update
  106.8 0.0 all-gather.10.cloned.1.call-start
  106.9 0.7 fusion.22
  108.9 0.1 copy.30
  109.7 24.4 %all-gather.8.cloned.1.call-done = f32[8,128,256]{2,1,0:T(8,128)} async-done(((f32[1,128,256]{2,1,0:T(8,128)}), f32[8,128,256]{2,1,0:T(8,128)}) %all-gather.8.cloned.1.call-update) | async-done | bytes 1048592 | tf_op jit(solution)/shard_map/all_gather | solution.py:29
  134.0 0.9 constant_dynamic-slice_fusion
  134.9 0.1 copy.44
  135.0 0.7 bitcast_convert_fusion
  135.7 0.0 all-gather.10.cloned.1.call-update
  135.7 0.0 all-gather.12.cloned.1.call-start
  136.5 0.2 select_reduce_fusion
  136.7 79.2 %all-gather.10.cloned.1.call-done = bf16[16384,256]{0,1:T(8,128)(2,1)} async-done(((bf16[128,256]{0,1:T(8,128)(2,1)}), bf16[16384,256]{0,1:T(8,128)(2,1)}) %all-gather.10.cloned.1.call-update) | async-done | bytes 8388624 | tf_op jit(solution)/shard_map/all_gather | solution.py:41
  215.8 11.6 %copy.41 = bf16[16384,256]{1,0:T(8,128)(2,1)} copy(bf16[16384,256]{0,1:T(8,128)(2,1)} %all-gather.10.cloned.1.call-done) | data formatting | bytes 16777216 | tf_op jit(solution)/shard_map/reshape | solution.py:42
  227.4 4.0 gather_fusion
  231.4 1.2 fusion.29
  232.6 0.0 all-gather.14.cloned.1.call-start
  232.6 79.0 %all-gather.12.cloned.1.call-done = bf16[16384,256]{0,1:T(8,128)(2,1)} async-done(((bf16[128,256]{0,1:T(8,128)(2,1)}), bf16[16384,256]{0,1:T(8,128)(2,1)}) %all-gather.12.cloned.1.call-update) | async-done | bytes 8388624 | tf_op jit(solution)/shard_map/all_gather | solution.py:41
  311.6 11.6 %copy.42 = bf16[16384,256]{1,0:T(8,128)(2,1)} copy(bf16[16384,256]{0,1:T(8,128)(2,1)} %all-gather.12.cloned.1.call-done) | data formatting | bytes 16777216 | tf_op jit(solution)/shard_map/reshape | solution.py:42
  323.2 4.0 gather_fusion.1
  327.2 1.2 fusion.30
  328.4 79.0 %all-gather.14.cloned.1.call-done = bf16[16384,256]{0,1:T(8,128)(2,1)} async-done(((bf16[128,256]{0,1:T(8,128)(2,1)}), bf16[16384,256]{0,1:T(8,128)(2,1)}) %all-gather.14.cloned.1.call-update) | async-done | bytes 8388624 | tf_op jit(solution)/shard_map/all_gather | solution.py:41
  407.4 11.6 %copy.43 = bf16[16384,256]{1,0:T(8,128)(2,1)} copy(bf16[16384,256]{0,1:T(8,128)(2,1)} %all-gather.14.cloned.1.call-done) | data formatting | bytes 16777216 | tf_op jit(solution)/shard_map/reshape | solution.py:42
  419.0 4.0 gather_fusion.2
  423.0 0.5 fusion.9
  423.5 0.8 copy.37
  (15 shorter events, 0.1 us)
Async XLA Ops:
  6.5 224.9 %copy-start = (bf16[12,128,128]{2,1,0:T(8,128)(2,1)S(1)}, bf16[12,128,128]{2,1,0:T(8,128)(2,1)}, u32[]{:S(2)}) copy-start(bf16[12,128,128]{2,1,0:T(8,128)(2,1)} %param.14) | copy-start | bytes 1179652
  6.5 60.3 %all-gather.6.cloned.1.call-start = ((), (), s32[]{:S(2)}) async-start(), calls=%async_computation.1 | async-start | bytes 5013504 | tf_op jit(solution)/shard_map/all_gather | solution.py:19
  7.3 99.6 %copy-start.2 = (s32[128]{0:T(128)S(1)}, s32[128]{0:T(128)}, u32[]{:S(2)}) copy-start(s32[128]{0:T(128)} %param.12) | copy-start | bytes 1540
  7.3 101.6 %copy-start.1 = (f32[1,128,256]{2,1,0:T(8,128)S(1)}, f32[1,128,256]{2,1,0:T(8,128)}, u32[]{:S(2)}) copy-start(f32[1,128,256]{2,1,0:T(8,128)} %param.11) | copy-start | bytes 393220
  7.3 129.2 %copy-start.3 = (s32[12,2]{0,1:T(2,128)S(1)}, s32[12,2]{0,1:T(2,128)}, u32[]{:S(2)}) copy-start(s32[12,2]{0,1:T(2,128)} %param.13) | copy-start | bytes 292
  7.3 99.5 %reduce-scatter.2.cloned.1.call-start = ((), (), s32[]{:S(2)}) async-start(), calls=%async_computation.2 | async-start | bytes 1179648 | tf_op jit(solution)/shard_map/reduce_scatter | solution.py:28
  78.0 56.0 %all-gather.8.cloned.1.call-start = ((), (), s32[]{:S(2)}) async-start(), calls=%async_computation.3 | async-start | bytes 1179648 | tf_op jit(solution)/shard_map/all_gather | solution.py:29
  106.8 109.0 %all-gather.10.cloned.1.call-start = ((), (), s32[]{:S(2)}) async-start(), calls=%async_computation.4 | async-start | bytes 8454144 | tf_op jit(solution)/shard_map/all_gather | solution.py:41
  135.7 175.9 %all-gather.12.cloned.1.call-start = ((), (), s32[]{:S(2)}) async-start(), calls=%async_computation.5 | async-start | bytes 8454144 | tf_op jit(solution)/shard_map/all_gather | solution.py:41
  232.6 174.8 %all-gather.14.cloned.1.call-start = ((), (), s32[]{:S(2)}) async-start(), calls=%async_computation.6 | async-start | bytes 8454144 | tf_op jit(solution)/shard_map/all_gather | solution.py:41
Sparse Core Ops, SparseCore 0:
  9.5 57.3 all-gather.5
  78.1 28.6 reduce-scatter.1
  108.5 25.4 all-gather.7
  136.7 79.0 all-gather.9
  232.7 78.8 all-gather.11
  328.5 78.8 all-gather.13
where the time goes:
time: 432 us; the launch traced here: 431 us
  waiting for transfers between devices  351 us (81%)
  local copies, waits for them, and re-layouts  48.5 us (11%)
  between operations  16.2 us (4%)
  matrix products  14 us (3%)
    all_gather x3, waiting for transfers between devices, per_device(): gathered = lax.all_gather(rounded, ('row', 'col'), axis=0, tiled=True)  237 us
    all_gather x1, waiting for transfers between devices, per_device(): lax.all_gather(history, 'col', axis=1, tiled=True)  59.5 us
    reshape x3, local copies, waits for them, and re-layouts, per_device(): gathered = gathered.reshape(-1, cluster, columns)  34.8 us
    reduce_scatter x1, waiting for transfers between devices, per_device(): block_sum = lax.psum_scatter(blocks, 'row', scatter_dimension=0, tiled=True)  28.8 us
    all_gather x1, waiting for transfers between devices, per_device(): everyone = lax.all_gather(block_sum, 'row', axis=0, tiled=True)  24.4 us
    gather x3, local copies, waits for them, and re-layouts, per_device(): picked = jnp.take(gathered, src_slot, axis=0)  11.9 us
    dot_general x1, matrix products, per_device(): lax.dot_general(kernels, lax.all_gather(history, 'col', axis=1, tiled=Tru...  11.1 us
  transfers between devices with their start and end apart: 6, of which 6 were waited for; matrix products, arithmetic and copies ran while one was open for 0% of the time, Pallas kernels for 0%

commit v1 on v0

v1 whole, which is shorter than its diff:
```python
import functools

import jax
import jax.numpy as jnp
from jax import lax
from jax.experimental import pallas as pl
from jax.experimental.pallas import tpu as pltpu
from jax.sharding import PartitionSpec as P

MESH = pl.DeviceIdType.MESH
F32, BF16 = jnp.float32, jnp.bfloat16

SWEEPS = 3
DAMPING = 0.7

NX, NZ, NY = 4, 4, 4
LAGS, SRC, COLS, CL = 6, 96, 256, 128
HALVES = 2
W = COLS // HALVES
LH = LAGS // 2
DEPTH = LH * NZ * SRC
TILES = 12
TM = 512


def body(kernels, history, incident, owner, pairs, tiles, counts, out,
         hb, kb, acc, sp, rp, ts, rf, ry, inc, drv, den, tl, tcat, gat00, gat01, gat02, gat10, gat11, gat12, owner_s, pairs_s, counts_s,
         lsem, ksem, hsem, gsem, gsend, psem, psend, ysem, ysend, ssem, ssend, osem):
    row, col = lax.axis_index("row"), lax.axis_index("col")
    y, core = lax.div(row, 2), lax.rem(row, 2)
    x, z = lax.div(col, NZ), lax.rem(col, NZ)
    other = 1 - core

    def at_col(dx, dz):
        return lax.rem(x + dx + NX, NX) * NZ + lax.rem(z + dz + NZ, NZ)

    def at_row(dy):
        return lax.rem(y + dy + NY, NY) * 2 + core

    def near_col(dc):
        return lax.rem(col + dc + NX * NZ, NX * NZ)

    def send(src, dst, ssem_, rsem_, r, c):
        pltpu.make_async_remote_copy(
            src_ref=src, dst_ref=dst, send_sem=ssem_, recv_sem=rsem_,
            device_id={"row": r, "col": c}, device_id_type=MESH,
        ).start()

    def wait(ref, sem):
        pltpu.make_async_copy(ref, ref, sem).wait()

    gat = ((gat00, gat01, gat02), (gat10, gat11, gat12))

    barrier = pltpu.get_barrier_semaphore()
    greet = [(row, at_col(1, 0)), (row, at_col(-1, 0)), (row, at_col(0, 1)), (row, at_col(0, -1))]
    greet += [(at_row(dy), near_col(dc)) for dy in (-1, 0, 1) for dc in (-1, 0, 1) if dy or dc]
    greet += [(y * 2 + other, col)]
    for r, c in greet:
        pl.semaphore_signal(barrier, inc=1, device_id={"row": r, "col": c}, device_id_type=MESH)

    def piece(h, a, dx, dz, lo=0, n=SRC):
        zr = pl.multiple_of(lax.rem(z + dz + NZ, NZ) * SRC + lo, 16)
        return hb.at[h, a, dx % NX, :, pl.ds(zr, n), :]

    def own(h, a):
        return history.at[pl.ds(a * LH, LH), :, pl.ds(h * W, W)]

    for h in range(HALVES):
        for a in range(2):
            pltpu.make_async_copy(own(h, a), piece(h, a, 0, 0), hsem.at[h, a]).start()
    pltpu.make_async_copy(owner, owner_s, lsem.at[0]).start()
    pltpu.make_async_copy(pairs, pairs_s, lsem.at[1]).start()
    pltpu.make_async_copy(counts, counts_s, lsem.at[2]).start()
    pl.semaphore_wait(barrier, len(greet))

    events = []

    def at(t):
        def add(f):
            events.append((t, len(events), f))
        return add

    def axis(a, phase):
        return ((1, 0), (0, 1))[(a + phase) % 2]

    def move(h, a, off, d, lo, n, sem, first=False):
        src = own(h, a) if first else piece(h, a, off[0], off[1], lo, n)
        zr = pl.multiple_of(lax.rem(z + off[1] + NZ, NZ) * SRC + lo, 16)
        dst = hb.at[h, a, (off[0] - d[0]) % NX, :, pl.ds(zr, n), :]
        send(src, dst, gsend.at[h, 0 if d[0] else 1], sem, row, at_col(d[0], d[1]))

    def neg(d):
        return (-d[0], -d[1])

    def mul(d, k):
        return (d[0] * k, d[1] * k)

    def add2(p, q):
        return (p[0] + q[0], p[1] + q[1])

    half = SRC // 2

    def spread(h, a, off, j, first=False):
        d = axis(a, 1)
        move(h, a, off, d, 0, SRC, gsem.at[h, a, j, 0], first)
        move(h, a, off, neg(d), 0, SRC, gsem.at[h, a, j, 1], first)

    def relay(h, a, off, j, d):
        lo, hi = add2(off, neg(d)), add2(off, d)
        wait(piece(h, a, *lo), gsem.at[h, a, j, 0])
        move(h, a, lo, d, 0, half, gsem.at[h, a, j, 2])
        wait(piece(h, a, *hi), gsem.at[h, a, j, 1])
        move(h, a, hi, neg(d), half, half, gsem.at[h, a, j, 3])

    def far(h, a, off, j, d):
        o = add2(off, mul(d, 2))
        wait(piece(h, a, o[0], o[1], 0, half), gsem.at[h, a, j, 2])
        wait(piece(h, a, o[0], o[1], half, half), gsem.at[h, a, j, 3])

    started = [False] * HALVES
    kwaited = set()

    def mm(h, a, dx):
        g = a * NX + dx % NX
        if g not in kwaited:
            kwaited.add(g)
            for l in range(LH):
                wait(kb.at[g, :, pl.ds(l * NZ * SRC, NZ * SRC)], ksem.at[g, l])
        first = not started[h]
        started[h] = True

        def step(i, carry):
            rows = pl.ds(pl.multiple_of(i * TM, TM), TM)
            blocks = pl.ds(i * (TM // CL), TM // CL)
            d = jnp.dot(kb[g, rows, :], hb[h, a, dx % NX].reshape(DEPTH, W), preferred_element_type=F32)
            d = d.reshape(TM // CL, CL, W)
            acc[h, blocks] = d if first else acc[h, blocks] + d
            return carry

        lax.fori_loop(0, NX * NZ // 2 * CL // TM, step, 0)

    def gather(h, t0, u):
        @at(t0)
        def _():
            for a in range(2):
                d = axis(a, 0)
                move(h, a, (0, 0), d, 0, SRC, gsem.at[h, a, 0, 0], True)
                move(h, a, (0, 0), neg(d), 0, SRC, gsem.at[h, a, 0, 1], True)
            for a in range(2):
                spread(h, a, (0, 0), 1, True)
            if h == 0:
                order = [(1, 0), (0, 0), (1, 3), (1, 1), (0, 3), (0, 1), (0, 2), (1, 2)]
                for a, rel in order:
                    gx = lax.rem(x + rel, NX)
                    for l in range(LH):
                        pltpu.make_async_copy(
                            kernels.at[a * LH + l, :, pl.ds(pl.multiple_of(gx * (NZ * SRC), 128), NZ * SRC)],
                            kb.at[a * NX + rel, :, pl.ds(l * NZ * SRC, NZ * SRC)],
                            ksem.at[a * NX + rel, l],
                        ).start()
                pltpu.make_async_copy(incident, inc, lsem.at[3]).start()
                pltpu.make_async_copy(tiles, tl, lsem.at[4]).start()

        @at(t0 + 1.2 * u)
        def _():
            for a in range(2):
                p = axis(a, 0)
                relay(h, a, (0, 0), 0, p)
            for a in range(2):
                p = axis(a, 0)
                spread(h, a, neg(p), 2)
                spread(h, a, p, 3)

        @at(t0 + 2.2 * u)
        def _():
            for a in range(2):
                relay(h, a, (0, 0), 1, axis(a, 1))

        @at(t0 + 2.7 * u)
        def _():
            for a in range(2):
                p = axis(a, 0)
                far(h, a, (0, 0), 0, p)
                spread(h, a, mul(p, 2), 4)
            for a in range(2):
                wait(piece(h, a, 0, 0), hsem.at[h, a])
            mm(h, 1, 0)

        @at(t0 + 3.7 * u)
        def _():
            for a in range(2):
                relay(h, a, neg(axis(a, 0)), 2, axis(a, 1))

        @at(t0 + 4.7 * u)
        def _():
            for a in range(2):
                relay(h, a, axis(a, 0), 3, axis(a, 1))

        @at(t0 + 5.2 * u)
        def _():
            for a in range(2):
                far(h, a, (0, 0), 1, axis(a, 1))
            mm(h, 0, 0)

        @at(t0 + 6.2 * u)
        def _():
            for a in range(2):
                relay(h, a, mul(axis(a, 0), 2), 4, axis(a, 1))

        @at(t0 + 6.3 * u)
        def _():
            mm(h, 1, -1)

        @at(t0 + 6.5 * u)
        def _():
            mm(h, 1, 1)

        @at(t0 + 6.8 * u)
        def _():
            for a in range(2):
                far(h, a, neg(axis(a, 0)), 2, axis(a, 1))
            mm(h, 0, -1)

        @at(t0 + 7.3 * u)
        def _():
            for a in range(2):
                far(h, a, axis(a, 0), 3, axis(a, 1))
            mm(h, 0, 1)

        @at(t0 + 7.8 * u)
        def _():
            for a in range(2):
                far(h, a, mul(axis(a, 0), 2), 4, axis(a, 1))
            mm(h, 0, 2)
            mm(h, 1, 2)

    tab = {}

    def position(r):
        p = jnp.int32(0)
        for b in range(NY * 2):
            p = p + jnp.where(owner_s[col * (NY * 2) + b] == r, b, 0)
        return jnp.minimum(p, NY * 2 - 1)

    def summed(h, t0, gap):
        hh = CL // 2

        @at(t0)
        def _():
            if "pos" not in tab:
                wait(owner_s, lsem.at[0])
                tab["pos"] = {dy: position(at_row(dy)) for dy in (0, 1, 2, 3)}
                tab["oth"] = {dy: position(at_row(dy) + other - core) for dy in (0, 1, 2, 3)}
            for i, dy in enumerate((2, 1, 3, 0)):
                sp[h, i] = acc[h, tab["oth"][dy]]
                send(sp.at[h, i], rp.at[h, i], psend.at[h], psem.at[h, i], y * 2 + other, col)

        @at(t0 + gap)
        def _():
            wait(rp.at[h, 0], psem.at[h, 0])
            ts[h, 0] = acc[h, tab["pos"][2]] + rp[h, 0]
            send(ts.at[h, 0, pl.ds(0, hh)], rf.at[h, 0], ysend.at[h], ysem.at[h, 0], at_row(1), col)
            send(ts.at[h, 0, pl.ds(hh, hh)], rf.at[h, 1], ysend.at[h], ysem.at[h, 1], at_row(-1), col)
            wait(rp.at[h, 1], psem.at[h, 1])
            ts[h, 1] = acc[h, tab["pos"][1]] + rp[h, 1]
            send(ts.at[h, 1, pl.ds(hh, hh)], ry.at[h, 0, pl.ds(hh, hh)], ysend.at[h], ysem.at[h, 2], at_row(1), col)
            wait(rp.at[h, 2], psem.at[h, 2])
            ts[h, 2] = acc[h, tab["pos"][3]] + rp[h, 2]
            send(ts.at[h, 2, pl.ds(0, hh)], ry.at[h, 1, pl.ds(0, hh)], ysend.at[h], ysem.at[h, 3], at_row(-1), col)
            wait(rp.at[h, 3], psem.at[h, 3])
            if h == 0:
                wait(inc, lsem.at[3])
            drv[h] = inc[0, :, pl.ds(h * W, W)] - (acc[h, tab["pos"][0]] + rp[h, 3])

        @at(t0 + 2 * gap)
        def _():
            wait(rf.at[h, 0], ysem.at[h, 0])
            ts[h, 1, pl.ds(0, hh)] += rf[h, 0]
            send(ts.at[h, 1, pl.ds(0, hh)], ry.at[h, 0, pl.ds(0, hh)], ysend.at[h], ysem.at[h, 4], at_row(1), col)
            wait(rf.at[h, 1], ysem.at[h, 1])
            ts[h, 2, pl.ds(hh, hh)] += rf[h, 1]
            send(ts.at[h, 2, pl.ds(hh, hh)], ry.at[h, 1, pl.ds(hh, hh)], ysend.at[h], ysem.at[h, 5], at_row(-1), col)

        @at(t0 + 3 * gap)
        def _():
            wait(ry.at[h, 0, pl.ds(hh, hh)], ysem.at[h, 2])
            wait(ry.at[h, 1, pl.ds(0, hh)], ysem.at[h, 3])
            wait(ry.at[h, 0, pl.ds(0, hh)], ysem.at[h, 4])
            wait(ry.at[h, 1, pl.ds(hh, hh)], ysem.at[h, 5])
            drv[h] = drv[h] - (ry[h, 0] + ry[h, 1])

    def slots():
        if "slots" not in tab:
            wait(pairs_s, lsem.at[1])
            made = []
            for t in range(TILES):
                s = jnp.clip(pairs_s[1, t], 0, CL - 1)
                zi = jnp.minimum(lax.rem(lax.shift_right_logical(s, 3) - col + 2 * NX * NZ + 1, NX * NZ), 2)
                made.append((zi, jnp.clip(owner_s[s], 0, 2 * NY - 1)))
            tab["slots"] = made
        return tab["slots"]

    @at(3.0)
    def _():
        wait(tl, lsem.at[4])
        wait(counts_s, lsem.at[2])
        for t in range(TILES):
            tcat[:, pl.ds(t * CL, CL)] = jnp.where(t < counts_s[0], tl[t], jnp.zeros((), BF16))

    def sweep(h, s, t0, gap):
        g = gat[h][s]
        up, down, over = at_row(1), at_row(-1), at_row(2)
        hh = CL // 2

        @at(t0)
        def _():
            cur = drv[h] if s == 0 else den[h]
            g[1, row] = cur.astype(BF16)
            src = g.at[1, row]
            for dc, zi in ((1, 0), (-1, 2), (0, 1)):
                send(src, g.at[zi, row], ssend.at[h, s, 0], ssem.at[h, s, 1], up, near_col(dc))
                send(src, g.at[zi, row], ssend.at[h, s, 0], ssem.at[h, s, 2], down, near_col(dc))
            for dc, zi in ((1, 0), (-1, 2)):
                send(src, g.at[zi, row], ssend.at[h, s, 0], ssem.at[h, s, 0], row, near_col(dc))

        def cross(r, i):
            send(g.at[:, r], g.at[:, r], ssend.at[h, s, 1], ssem.at[h, s, i], y * 2 + other, col)

        @at(t0 + gap)
        def _():
            wait(g.at[:, down], ssem.at[h, s, 1])
            send(g.at[:, down, pl.ds(0, hh)], g.at[:, down, pl.ds(0, hh)], ssend.at[h, s, 1], ssem.at[h, s, 3], up, col)
            wait(g.at[:, up], ssem.at[h, s, 2])
            send(g.at[:, up, pl.ds(hh, hh)], g.at[:, up, pl.ds(hh, hh)], ssend.at[h, s, 1], ssem.at[h, s, 4], down, col)
            wait(g.at[pl.ds(0, 2), row], ssem.at[h, s, 0])
            cross(row, 5)
            cross(down, 6)
            cross(up, 7)

        @at(t0 + 2 * gap)
        def _():
            wait(g.at[:, over, pl.ds(0, hh)], ssem.at[h, s, 3])
            wait(g.at[:, over, pl.ds(hh, hh)], ssem.at[h, s, 4])
            cross(over, 8)

        @at(t0 + 3 * gap)
        def _():
            for i, r in ((5, row), (6, down), (7, up), (8, over)):
                wait(g.at[:, r + other - core], ssem.at[h, s, i])
            picked = jnp.concatenate([g[zi, r] for zi, r in slots()], axis=0)
            near = jnp.dot(tcat[...], picked, preferred_element_type=F32)
            d = drv[h]
            cur = d if s == 0 else den[h]
            den[h] = cur + DAMPING * (d - cur - near)
            if s == SWEEPS - 1:
                pltpu.make_async_copy(den.at[h], out.at[0, :, pl.ds(h * W, W)], osem.at[h]).start()

    U = 1.5
    T1 = 7.6
    gather(0, 0.0, U)
    summed(0, 13.0, 1.4)
    for s in range(SWEEPS):
        sweep(0, s, 17.5 + 4.6 * s, 1.5)
    gather(1, T1, U)
    summed(1, T1 + 14.0, 1.4)
    for s in range(SWEEPS):
        sweep(1, s, T1 + 18.3 + 4.6 * s, 1.5)

    for _, _, f in sorted(events, key=lambda e: e[:2]):
        f()

    for h in range(HALVES):
        for d in range(2):
            wait(hb.at[h, :, pl.ds(0, 3), :, pl.ds(0, 240), :], gsend.at[h, d])
        wait(sp.at[h], psend.at[h])
        wait(ts.at[h], ysend.at[h])
        for s in range(SWEEPS):
            wait(gat[h][s].at[0], ssend.at[h, s, 0])
            wait(gat[h][s].at[:, pl.ds(0, 5)], ssend.at[h, s, 1])
    for h in range(HALVES):
        wait(den.at[h], osem.at[h])


def per_device(kernels, history, incident, owner, pairs, tiles, counts):
    dma = pltpu.SemaphoreType.DMA
    any_ = pl.BlockSpec(memory_space=pl.ANY)
    return pl.pallas_call(
        body,
        out_shape=jax.ShapeDtypeStruct(incident.shape, F32),
        in_specs=[any_] * 7,
        out_specs=any_,
        scratch_shapes=[
            pltpu.VMEM((HALVES, 2, NX, LH, NZ * SRC, W), BF16),
            pltpu.VMEM((2 * NX, 8 * CL, DEPTH), BF16),
            pltpu.VMEM((HALVES, 8, CL, W), F32),
            pltpu.VMEM((HALVES, 4, CL, W), F32),
            pltpu.VMEM((HALVES, 4, CL, W), F32),
            pltpu.VMEM((HALVES, 3, CL, W), F32),
            pltpu.VMEM((HALVES, 2, CL // 2, W), F32),
            pltpu.VMEM((HALVES, 2, CL, W), F32),
            pltpu.VMEM((1, CL, COLS), F32),
            pltpu.VMEM((HALVES, CL, W), F32),
            pltpu.VMEM((HALVES, CL, W), F32),
            pltpu.VMEM((TILES, CL, CL), BF16),
            pltpu.VMEM((CL, TILES * CL), BF16),
            *[pltpu.VMEM((3, 8, CL, W), BF16)] * (HALVES * SWEEPS),
            pltpu.SMEM((128,), jnp.int32),
            pltpu.SMEM((2, TILES), jnp.int32),
            pltpu.SMEM((1,), jnp.int32),
            dma((5,)), dma((8, LH)), dma((HALVES, 2)), dma((HALVES, 2, 5, 4)), dma((HALVES, 2)),
            dma((HALVES, 4)), dma((HALVES,)), dma((HALVES, 6)), dma((HALVES,)),
            dma((HALVES, SWEEPS, 9)), dma((HALVES, SWEEPS, 2)), dma((HALVES,)),
        ],
        compiler_params=pltpu.CompilerParams(
            collective_id=0, has_side_effects=True, vmem_limit_bytes=56 * 2**20
        ),
        cost_estimate=pl.CostEstimate(flops=5_200_000_000, bytes_accessed=21_000_000, transcendentals=0),
    )(kernels, history, incident, owner, pairs.T, tiles, counts)


def solution(mesh):
    both = ("row", "col")
    in_specs = (
        P(None, "col", "row"), P(None, both, None), P(both, None, None), P(),
        P(both, None), P(both, None, None), P(both),
    )
    return jax.shard_map(
        per_device, mesh=mesh, in_specs=in_specs, out_specs=P(both, None, None), check_vma=False
    )
```

time: 432 us -> 98.6 us (0.23)
  waiting for transfers between devices: 351 us -> 0 us
  Pallas kernels: 0 us -> 95.5 us
  local copies, waits for them, and re-layouts: 48.5 us -> 1.57 us
  between operations: 16.2 us -> 0.66 us
  matrix products: 14 us -> 0 us
    all_gather x5 -> x0, waiting for transfers between devices: 321 us -> none  [the longest x3 237 us: per_device(): gathered = lax.all_gather(rounded, ('row', 'col'), axis=0, tiled=True)]
    pallas_call x0 -> x1, Pallas kernels: none -> 95.5 us  [per_device(): pl.pallas_call(body, out_shape=jax.ShapeDtypeStruct(incident.shape, F32),...]
    reshape x3 -> x0, local copies, waits for them, and re-layouts: 34.8 us -> none  [per_device(): gathered = gathered.reshape(-1, cluster, columns)]
    reduce_scatter x1 -> x0, waiting for transfers between devices: 28.8 us -> none  [per_device(): block_sum = lax.psum_scatter(blocks, 'row', scatter_dimension=0, tiled=True)]
    dot_general x4 -> x0, matrix products: 14 us -> none  [the longest x1 11.1 us: per_device(): lax.dot_general(kernels, lax.all_gather(history, 'col', axis=1, tiled=Tru...]
    gather x3 -> x0, local copies, waits for them, and re-layouts: 11.9 us -> none  [per_device(): picked = jnp.take(gathered, src_slot, axis=0)]
  transfers between devices with their start and end apart: 6 -> 0, of which waited for: 6 -> 0; matrix products, arithmetic and copies ran while one was open for 0% -> 0% of each run, Pallas kernels for 0% -> 0%
where the time goes in v1:
time: 98.6 us; the launch traced here: 97.7 us
  Pallas kernels  95.5 us (97%)
  local copies, waits for them, and re-layouts  1.57 us (2%)
    pallas_call x1, Pallas kernels, per_device(): pl.pallas_call(body, out_shape=jax.ShapeDtypeStruct(incident.shape, F32),...  95.5 us

profile of v1, /device:TPU:1, one launch (start us, length us, event | category | flops | bytes accessed | tf_op | source)
XLA Modules:
  0.0 97.7 jit_solution(1747528835633263704)
XLA Ops:
  0.7 95.5 %shard_map.73 = f32[1,128,256]{2,1,0:T(8,128)} custom-call(bf16[6,1024,1536]{2,1,0:T(8,128)(2,1)} %kernels.1, bf16[6,96,256]{2,1,0:T(8,128)(2,1)} %history.1, f32[1,128,256]{2,1,0:T(8,128)} %incident.1, s32[128]{0:T(128)} %owner.1, s32[2,12]{1,0:T(2,128)} %bitcast.1, bf16[12,128,128]{2,1,0:T(8,128)(2,1)} %tiles.1, s32[1]{0:T(128)S(6)} %copy.9.counts), custom_call_target="tpu_custom_call" | custom-call | flops 5200000000 | bytes 21000000 | tf_op jit(solution)/shard_map/pallas_call | solution.py:387
  96.2 1.6 %copy.10 = f32[1,128,256]{2,1,0:T(8,128)} copy(f32[1,128,256]{2,1,0:T(8,128)} %shard_map.73) | data formatting | bytes 262144

commit v2 on v1

v2 whole, which is shorter than its diff:
```python
import functools

import jax
import jax.numpy as jnp
from jax import lax
from jax.experimental import pallas as pl
from jax.experimental.pallas import tpu as pltpu
from jax.sharding import PartitionSpec as P

MESH = pl.DeviceIdType.MESH
F32, BF16 = jnp.float32, jnp.bfloat16

SWEEPS = 3
DAMPING = 0.7

NX, NZ, NY = 4, 4, 4
LAGS, SRC, COLS, CL = 6, 96, 256, 128
HALVES = 2
W = COLS // HALVES
LH = LAGS // 2
DEPTH = LH * NZ * SRC
TILES = 12


def body(kernels, history, incident, owner, pairs, tiles, counts, out,
         hb, kb, acc, mine, sp, rp, ts, ry, inc, drv, den, fin, last, tl, wt,
         gat00, gat01, gat02, gat10, gat11, gat12, owner_s, pairs_s, counts_s, codes,
         lsem, ksem, hsem, gsem, gsend, bsem, bsend, psem, psend, ysem, ysend, ssem, ssend, fsem, fsend, osem):
    row, col = lax.axis_index("row"), lax.axis_index("col")
    y, core = lax.div(row, 2), lax.rem(row, 2)
    x, z = lax.div(col, NZ), lax.rem(col, NZ)
    other = 1 - core

    def at_col(dx, dz):
        return lax.rem(x + dx + NX, NX) * NZ + lax.rem(z + dz + NZ, NZ)

    def at_row(dy):
        return lax.rem(y + dy + NY, NY) * 2 + core

    def near_col(dc):
        return lax.rem(col + dc + NX * NZ, NX * NZ)

    def send(src, dst, ssem_, rsem_, r, c):
        pltpu.make_async_remote_copy(
            src_ref=src, dst_ref=dst, send_sem=ssem_, recv_sem=rsem_,
            device_id={"row": r, "col": c}, device_id_type=MESH,
        ).start()

    def wait(ref, sem):
        pltpu.make_async_copy(ref, ref, sem).wait()

    gat = ((gat00, gat01, gat02), (gat10, gat11, gat12))

    barrier = pltpu.get_barrier_semaphore()
    greet = [(row, at_col(1, 0)), (row, at_col(-1, 0)), (row, at_col(0, 1)), (row, at_col(0, -1))]
    greet += [(at_row(1), col), (at_row(-1), col), (at_row(2), col), (y * 2 + other, col)]
    for r, c in greet:
        pl.semaphore_signal(barrier, inc=1, device_id={"row": r, "col": c}, device_id_type=MESH)

    def piece(h, a, dx, dz, lo=0, n=SRC):
        zr = pl.multiple_of(lax.rem(z + dz + NZ, NZ) * SRC + lo, 16)
        return hb.at[h, a, dx % NX, :, pl.ds(zr, n), :]

    def own(h, a):
        return history.at[pl.ds(a * LH, LH), :, pl.ds(h * W, W)]

    for h in range(HALVES):
        for a in range(2):
            pltpu.make_async_copy(own(h, a), piece(h, a, 0, 0), hsem.at[h, a]).start()
    pltpu.make_async_copy(owner, owner_s, lsem.at[0]).start()
    pltpu.make_async_copy(pairs, pairs_s, lsem.at[1]).start()
    pltpu.make_async_copy(counts, counts_s, lsem.at[2]).start()
    pl.semaphore_wait(barrier, len(greet))
    mate = y * 2 + other

    events = []

    def at(t):
        def add(f):
            events.append((t, len(events), f))
        return add

    def axis(a, phase):
        return ((1, 0), (0, 1))[(a + phase) % 2]

    def move(h, a, off, d, lo, n, sem, first=False):
        src = own(h, a) if first else piece(h, a, off[0], off[1], lo, n)
        zr = pl.multiple_of(lax.rem(z + off[1] + NZ, NZ) * SRC + lo, 16)
        dst = hb.at[h, a, (off[0] - d[0]) % NX, :, pl.ds(zr, n), :]
        send(src, dst, gsend.at[h, 0 if d[0] else 1], sem, row, at_col(d[0], d[1]))

    def neg(d):
        return (-d[0], -d[1])

    def mul(d, k):
        return (d[0] * k, d[1] * k)

    def add2(p, q):
        return (p[0] + q[0], p[1] + q[1])

    half = SRC // 2

    def spread(h, a, off, j, first=False):
        d = axis(a, 1)
        move(h, a, off, d, 0, SRC, gsem.at[h, a, j, 0], first)
        move(h, a, off, neg(d), 0, SRC, gsem.at[h, a, j, 1], first)

    def relay(h, a, off, j, d):
        lo, hi = add2(off, neg(d)), add2(off, d)
        wait(piece(h, a, *lo), gsem.at[h, a, j, 0])
        move(h, a, lo, d, 0, half, gsem.at[h, a, j, 2])
        wait(piece(h, a, *hi), gsem.at[h, a, j, 1])
        move(h, a, hi, neg(d), half, half, gsem.at[h, a, j, 3])

    def far(h, a, off, j, d):
        o = add2(off, mul(d, 2))
        wait(piece(h, a, o[0], o[1], 0, half), gsem.at[h, a, j, 2])
        wait(piece(h, a, o[0], o[1], half, half), gsem.at[h, a, j, 3])

    order = [(1, 0), (0, 0), (1, 3), (1, 1), (0, 3), (0, 1), (1, 2), (0, 2)]

    def mm(a, dx):
        g = a * NX + dx % NX
        for l in range(LH):
            wait(kb.at[g, :, pl.ds(l * NZ * SRC, NZ * SRC)], ksem.at[g, l])
        w = jnp.concatenate([hb[h, a, dx % NX].reshape(DEPTH, W) for h in range(HALVES)], axis=1)
        d = jnp.dot(kb[g], w, preferred_element_type=F32)
        for h in range(HALVES):
            part = d[:, h * W:(h + 1) * W].reshape(2 * NY, CL, W)
            acc[h] = part if (a, dx % NX) == order[0] else acc[h] + part

    def product(h, t0, a, dx):
        if h == HALVES - 1:
            @at(t0)
            def _():
                mm(a, dx)

    def gather(h, t0, u):
        @at(t0)
        def _():
            for a in range(2):
                d = axis(a, 0)
                move(h, a, (0, 0), d, 0, SRC, gsem.at[h, a, 0, 0], True)
                move(h, a, (0, 0), neg(d), 0, SRC, gsem.at[h, a, 0, 1], True)
            for a in range(2):
                spread(h, a, (0, 0), 1, True)

        @at(t0 + 1.2 * u)
        def _():
            for a in range(2):
                p = axis(a, 0)
                relay(h, a, (0, 0), 0, p)
            for a in range(2):
                p = axis(a, 0)
                spread(h, a, neg(p), 2)
                spread(h, a, p, 3)

        @at(t0 + 2.2 * u)
        def _():
            for a in range(2):
                relay(h, a, (0, 0), 1, axis(a, 1))

        @at(t0 + 2.7 * u)
        def _():
            for a in range(2):
                p = axis(a, 0)
                far(h, a, (0, 0), 0, p)
                spread(h, a, mul(p, 2), 4)
            for a in range(2):
                wait(piece(h, a, 0, 0), hsem.at[h, a])

        product(h, t0 + 2.7 * u, 1, 0)

        @at(t0 + 3.7 * u)
        def _():
            for a in range(2):
                relay(h, a, neg(axis(a, 0)), 2, axis(a, 1))

        @at(t0 + 4.7 * u)
        def _():
            for a in range(2):
                relay(h, a, axis(a, 0), 3, axis(a, 1))

        @at(t0 + 5.2 * u)
        def _():
            for a in range(2):
                far(h, a, (0, 0), 1, axis(a, 1))

        product(h, t0 + 5.2 * u, 0, 0)

        @at(t0 + 6.2 * u)
        def _():
            for a in range(2):
                relay(h, a, mul(axis(a, 0), 2), 4, axis(a, 1))

        product(h, t0 + 6.3 * u, 1, -1)

        product(h, t0 + 6.5 * u, 1, 1)

        @at(t0 + 6.8 * u)
        def _():
            for a in range(2):
                far(h, a, neg(axis(a, 0)), 2, axis(a, 1))

        product(h, t0 + 6.8 * u, 0, -1)

        @at(t0 + 7.3 * u)
        def _():
            for a in range(2):
                far(h, a, axis(a, 0), 3, axis(a, 1))

        product(h, t0 + 7.3 * u, 0, 1)

        @at(t0 + 7.8 * u)
        def _():
            far(h, 1, mul(axis(1, 0), 2), 4, axis(1, 1))

        product(h, t0 + 7.8 * u, 1, 2)

        @at(t0 + 7.8 * u)
        def _():
            far(h, 0, mul(axis(0, 0), 2), 4, axis(0, 1))

        product(h, t0 + 7.8 * u, 0, 2)

    tab = {}

    def position(r):
        p = jnp.int32(0)
        for b in range(NY * 2):
            p = p + jnp.where(owner_s[col * (NY * 2) + b] == r, b, 0)
        return jnp.minimum(p, NY * 2 - 1)

    low = lax.broadcasted_iota(jnp.int32, (CL, W), 1) < W // 2

    def pack(a, b):
        ra, rb = pltpu.roll(a, W // 2, 1), pltpu.roll(b, W // 2, 1)
        lo, hi = jnp.where(low, a, rb), jnp.where(low, ra, b)
        return jnp.where(core == 0, lo, hi), jnp.where(core == 0, hi, lo)

    def summed(h, t0, t1, t2):
        @at(t0)
        def _():
            if "pos" not in tab:
                tab["pos"] = {(dy, q): position(at_row(dy) - core + q) for dy in range(NY) for q in (0, 1)}
            for i, dy in enumerate((2, 1, 3, 0)):
                own_, theirs = pack(acc[h, tab["pos"][dy, 0]], acc[h, tab["pos"][dy, 1]])
                sp[h, i] = theirs
                send(sp.at[h, i], rp.at[h, i], psend.at[h], psem.at[h, i], mate, col)
                mine[h, i] = own_

        @at(t1)
        def _():
            for i, dy in enumerate((2, 1, 3)):
                wait(rp.at[h, i], psem.at[h, i])
                ts[h, i] = mine[h, i] + rp[h, i]
                send(ts.at[h, i], ry.at[h, i], ysend.at[h], ysem.at[h, i], at_row(dy), col)
            wait(rp.at[h, 3], psem.at[h, 3])
            if h == 0:
                wait(inc.at[core], lsem.at[3])
                wait(inc.at[other], bsem.at[0])
            cols = pl.ds(h * W, W)
            drv[h] = pack(inc[0, 0, :, cols], inc[1, 0, :, cols])[0] - (mine[h, 3] + rp[h, 3])

        @at(t2)
        def _():
            for i in (1, 2, 0):
                wait(ry.at[h, i], ysem.at[h, i])
            drv[h] = drv[h] - (ry[h, 0] + (ry[h, 1] + ry[h, 2]))

    @at(1.0)
    def _():
        wait(owner_s, lsem.at[0])
        wait(pairs_s, lsem.at[1])
        wait(counts_s, lsem.at[2])
        for t in range(TILES):
            s = jnp.clip(pairs_s[1, t], 0, CL - 1)
            zi = jnp.minimum(lax.rem(lax.shift_right_logical(s, 3) - col + 2 * NX * NZ + 1, NX * NZ), 2)
            codes[core, t] = jnp.where(t < counts_s[0], zi * (2 * NY) + owner_s[s], -1)
        for t in range(TILES, 16):
            codes[core, t] = -1
        send(codes.at[core], codes.at[core], bsend.at[2], bsem.at[2], mate, col)

    def weights(dy, t0):
        @at(t0)
        def _():
            if dy == 0:
                wait(codes.at[other], bsem.at[2])
                wait(tl.at[core], lsem.at[4])
                wait(tl.at[other], bsem.at[1])
            for k in range(2):
                c = [codes[k, t] for t in range(TILES)]
                for zi in range(3):
                    for q in range(2):
                        want = zi * (2 * NY) + at_row(dy) - core + q
                        found = jnp.int32(-1)
                        for t in range(TILES):
                            found = jnp.where(c[t] == want, t, found)
                        tile = tl[k, jnp.maximum(found, 0)]
                        wt[dy, pl.ds((k * 2 + q) * CL, CL), pl.ds(zi * CL, CL)] = jnp.where(
                            found >= 0, tile, jnp.zeros((), BF16))

    for dy in range(NY):
        weights(dy, 4.0 + 0.9 * dy)

    def sweep(h, s, t0, t1):
        g = gat[h][s]
        ys = [lax.rem(y + dy, NY) for dy in range(NY)]

        @at(t0)
        def _():
            cur = drv[h] if s == 0 else den[h]
            g[y, 1] = cur.astype(BF16)
            src = g.at[y, 1]
            for i in (2, 1, 3, 0):
                for dc, zi in ((1, 0), (-1, 2), (0, 1)):
                    if i or dc:
                        send(src, g.at[y, zi], ssend.at[h, s], ssem.at[h, s, i], at_row(-i), near_col(dc))

        @at(t1)
        def _():
            near = None
            for i in (0, 1, 3, 2):
                if i:
                    wait(g.at[ys[i]], ssem.at[h, s, i])
                else:
                    wait(g.at[y, pl.ds(0, 2)], ssem.at[h, s, 0])
                part = jnp.dot(wt[i], g[ys[i]].reshape(3 * CL, W), preferred_element_type=F32)
                near = part if near is None else near + part
            n00, n01, n10, n11 = (near[q * CL:(q + 1) * CL] for q in range(4))
            near = jnp.where(low, n00 + pltpu.roll(n01, W // 2, 1), pltpu.roll(n10, W // 2, 1) + n11)
            d = drv[h]
            cur = d if s == 0 else den[h]
            new = cur + DAMPING * (d - cur - near)
            if s < SWEEPS - 1:
                den[h] = new
            else:
                fin[h] = new
                send(fin.at[h], last.at[h], fsend.at[h], fsem.at[h], mate, col)

    def finish(h, t0):
        @at(t0)
        def _():
            wait(last.at[h], fsem.at[h])
            mine_, theirs = fin[h], pltpu.roll(last[h], W // 2, 1)
            den[h] = jnp.where(
                core == 0, jnp.where(low, mine_, theirs), jnp.where(low, theirs, mine_))
            pltpu.make_async_copy(den.at[h], out.at[0, :, pl.ds(h * W, W)], osem.at[h]).start()

    def loads():
        for a, rel in order:
            gx = lax.rem(x + rel, NX)
            for l in range(LH):
                pltpu.make_async_copy(
                    kernels.at[a * LH + l, :, pl.ds(pl.multiple_of(gx * (NZ * SRC), 128), NZ * SRC)],
                    kb.at[a * NX + rel, :, pl.ds(l * NZ * SRC, NZ * SRC)],
                    ksem.at[a * NX + rel, l],
                ).start()
        pltpu.make_async_copy(incident, inc.at[core], lsem.at[3]).start()
        pltpu.make_async_copy(tiles, tl.at[core], lsem.at[4]).start()
        send(incident, inc.at[core], bsend.at[0], bsem.at[0], mate, col)
        send(tiles, tl.at[core], bsend.at[1], bsem.at[1], mate, col)

    events.append((0.02, 1000, loads))

    gather(0, 0.0, 3.2)
    gather(1, 0.01, 3.2)
    summed(0, 30.0, 31.4, 36.5)
    summed(1, 30.1, 31.5, 38.5)
    ST0 = (36.6, 44.0, 51.5, 59.0)
    ST1 = (38.6, 46.0, 53.5, 61.0)
    for s in range(SWEEPS):
        sweep(0, s, ST0[s], ST0[s + 1] - 0.05)
        sweep(1, s, ST1[s], ST1[s + 1] - 0.05)
    finish(0, 60.0)
    finish(1, 62.0)

    for _, _, f in sorted(events, key=lambda e: e[:2]):
        f()

    wait(inc.at[core], bsend.at[0])
    wait(tl.at[core], bsend.at[1])
    wait(codes.at[core], bsend.at[2])
    for h in range(HALVES):
        for d in range(2):
            wait(hb.at[h, :, pl.ds(0, 3), :, pl.ds(0, 240), :], gsend.at[h, d])
        wait(sp.at[h], psend.at[h])
        wait(ts.at[h], ysend.at[h])
        for s in range(SWEEPS):
            wait(tl.at[0, pl.ds(0, NY * 3 - 1)], ssend.at[h, s])
        wait(fin.at[h], fsend.at[h])
        wait(den.at[h], osem.at[h])


def per_device(kernels, history, incident, owner, pairs, tiles, counts):
    dma = pltpu.SemaphoreType.DMA
    any_ = pl.BlockSpec(memory_space=pl.ANY)
    return pl.pallas_call(
        body,
        out_shape=jax.ShapeDtypeStruct(incident.shape, F32),
        in_specs=[any_] * 7,
        out_specs=any_,
        scratch_shapes=[
            pltpu.VMEM((HALVES, 2, NX, LH, NZ * SRC, W), BF16),
            pltpu.VMEM((2 * NX, 8 * CL, DEPTH), BF16),
            pltpu.VMEM((HALVES, 8, CL, W), F32),
            *[pltpu.VMEM((HALVES, 4, CL, W), F32)] * 3,
            *[pltpu.VMEM((HALVES, 3, CL, W), F32)] * 2,
            pltpu.VMEM((2, 1, CL, COLS), F32),
            *[pltpu.VMEM((HALVES, CL, W), F32)] * 4,
            pltpu.VMEM((2, TILES, CL, CL), BF16),
            pltpu.VMEM((NY, 4 * CL, 3 * CL), BF16),
            *[pltpu.VMEM((NY, 3, CL, W), BF16)] * (HALVES * SWEEPS),
            pltpu.SMEM((128,), jnp.int32),
            pltpu.SMEM((2, TILES), jnp.int32),
            pltpu.SMEM((1,), jnp.int32),
            pltpu.SMEM((2, 16), jnp.int32),
            dma((5,)), dma((8, LH)), dma((HALVES, 2)), dma((HALVES, 2, 5, 4)), dma((HALVES, 2)),
            dma((3,)), dma((3,)), dma((HALVES, 4)), dma((HALVES,)), dma((HALVES, 3)), dma((HALVES,)),
            dma((HALVES, SWEEPS, 4)), dma((HALVES, SWEEPS)), dma((HALVES,)), dma((HALVES,)), dma((HALVES,)),
        ],
        compiler_params=pltpu.CompilerParams(
            collective_id=0, has_side_effects=True, vmem_limit_bytes=56 * 2**20
        ),
        cost_estimate=pl.CostEstimate(flops=5_200_000_000, bytes_accessed=21_000_000, transcendentals=0),
    )(kernels, history, incident, owner, pairs.T, tiles, counts)


def solution(mesh):
    both = ("row", "col")
    in_specs = (
        P(None, "col", "row"), P(None, both, None), P(both, None, None), P(),
        P(both, None), P(both, None, None), P(both),
    )
    return jax.shard_map(
        per_device, mesh=mesh, in_specs=in_specs, out_specs=P(both, None, None), check_vma=False
    )
```

time: 98.6 us -> 80.9 us (0.82)
  Pallas kernels: 95.5 us -> 78.6 us
    pallas_call x1, Pallas kernels: 95.5 us -> 78.6 us  [per_device(): pl.pallas_call(body, out_shape=jax.ShapeDtypeStruct(incident.shape, F32),...]
where the time goes in v2:
time: 80.9 us; the launch traced here: 80.8 us
  Pallas kernels  78.6 us (97%)
  local copies, waits for them, and re-layouts  1.57 us (2%)
    pallas_call x1, Pallas kernels, per_device(): pl.pallas_call(body, out_shape=jax.ShapeDtypeStruct(incident.shape, F32),...  78.6 us

profile of v2, /device:TPU:1, one launch (start us, length us, event | category | flops | bytes accessed | tf_op | source)
XLA Modules:
  0.0 80.8 jit_solution(4014407028566467204)
XLA Ops:
  0.7 78.6 %shard_map.73 = f32[1,128,256]{2,1,0:T(8,128)} custom-call(bf16[6,1024,1536]{2,1,0:T(8,128)(2,1)} %kernels.1, bf16[6,96,256]{2,1,0:T(8,128)(2,1)} %history.1, f32[1,128,256]{2,1,0:T(8,128)} %incident.1, s32[128]{0:T(128)} %owner.1, s32[2,12]{1,0:T(2,128)} %bitcast.1, bf16[12,128,128]{2,1,0:T(8,128)(2,1)} %tiles.1, s32[1]{0:T(128)S(6)} %copy.9.counts), custom_call_target="tpu_custom_call" | custom-call | flops 5200000000 | bytes 21000000 | tf_op jit(solution)/shard_map/pallas_call | solution.py:398
  79.2 1.6 %copy.10 = f32[1,128,256]{2,1,0:T(8,128)} copy(f32[1,128,256]{2,1,0:T(8,128)} %shard_map.73) | data formatting | bytes 262144

commit v3 on v2

--- a/solution.py
+++ b/solution.py
@@ -17,15 +17,17 @@
 LAGS, SRC, COLS, CL = 6, 96, 256, 128
 HALVES = 2
 W = COLS // HALVES
+CW = COLS // 8
 LH = LAGS // 2
 DEPTH = LH * NZ * SRC
 TILES = 12
 
 
 def body(kernels, history, incident, owner, pairs, tiles, counts, out,
-         hb, kb, acc, mine, sp, rp, ts, ry, inc, drv, den, fin, last, tl, wt,
-         gat00, gat01, gat02, gat10, gat11, gat12, owner_s, pairs_s, counts_s, codes,
-         lsem, ksem, hsem, gsem, gsend, bsem, bsend, psem, psend, ysem, ysend, ssem, ssend, fsem, fsend, osem):
+         hb, kb, acc, mine, sp, rp, ts, ry, inc, ict, icd, drv, den, fin, last, res, tl,
+         gat0, gat1, gat2, owner_s, pairs_s, counts_s, codes,
+         lsem, ksem, hsem, gsem, gsend, tsem, tsend, isem, isend, csem, csend,
+         psem, psend, ysem, ysend, ssem, ssend, fsem, fsend, osem):
     row, col = lax.axis_index("row"), lax.axis_index("col")
     y, core = lax.div(row, 2), lax.rem(row, 2)
     x, z = lax.div(col, NZ), lax.rem(col, NZ)
@@ -49,7 +51,7 @@
     def wait(ref, sem):
         pltpu.make_async_copy(ref, ref, sem).wait()
 
-    gat = ((gat00, gat01, gat02), (gat10, gat11, gat12))
+    gat = (gat0, gat1, gat2)
 
     barrier = pltpu.get_barrier_semaphore()
     greet = [(row, at_col(1, 0)), (row, at_col(-1, 0)), (row, at_col(0, 1)), (row, at_col(0, -1))]
@@ -71,7 +73,6 @@
     pltpu.make_async_copy(pairs, pairs_s, lsem.at[1]).start()
     pltpu.make_async_copy(counts, counts_s, lsem.at[2]).start()
     pl.semaphore_wait(barrier, len(greet))
-    mate = y * 2 + other
 
     events = []
 
@@ -223,7 +224,13 @@
 
         product(h, t0 + 7.8 * u, 0, 2)
 
-    tab = {}
+    part = core * NY + y
+    peers = [(dy, flip) for dy in (2, 1, 3) for flip in (0, 1)] + [(0, 1)]
+
+    def peer(dy, flip):
+        y2 = lax.rem(y + dy, NY)
+        k2 = other if flip else core
+        return y2 * 2 + k2, k2 * NY + y2
 
     def position(r):
         p = jnp.int32(0)
@@ -231,44 +238,9 @@
             p = p + jnp.where(owner_s[col * (NY * 2) + b] == r, b, 0)
         return jnp.minimum(p, NY * 2 - 1)
 
-    low = lax.broadcasted_iota(jnp.int32, (CL, W), 1) < W // 2
-
-    def pack(a, b):
-        ra, rb = pltpu.roll(a, W // 2, 1), pltpu.roll(b, W // 2, 1)
-        lo, hi = jnp.where(low, a, rb), jnp.where(low, ra, b)
-        return jnp.where(core == 0, lo, hi), jnp.where(core == 0, hi, lo)
-
-    def summed(h, t0, t1, t2):
-        @at(t0)
-        def _():
-            if "pos" not in tab:
-                tab["pos"] = {(dy, q): position(at_row(dy) - core + q) for dy in range(NY) for q in (0, 1)}
-            for i, dy in enumerate((2, 1, 3, 0)):
-                own_, theirs = pack(acc[h, tab["pos"][dy, 0]], acc[h, tab["pos"][dy, 1]])
-                sp[h, i] = theirs
-                send(sp.at[h, i], rp.at[h, i], psend.at[h], psem.at[h, i], mate, col)
-                mine[h, i] = own_
-
-        @at(t1)
-        def _():
-            for i, dy in enumerate((2, 1, 3)):
-                wait(rp.at[h, i], psem.at[h, i])
-                ts[h, i] = mine[h, i] + rp[h, i]
-                send(ts.at[h, i], ry.at[h, i], ysend.at[h], ysem.at[h, i], at_row(dy), col)
-            wait(rp.at[h, 3], psem.at[h, 3])
-            if h == 0:
-                wait(inc.at[core], lsem.at[3])
-                wait(inc.at[other], bsem.at[0])
-            cols = pl.ds(h * W, W)
-            drv[h] = pack(inc[0, 0, :, cols], inc[1, 0, :, cols])[0] - (mine[h, 3] + rp[h, 3])
-
-        @at(t2)
-        def _():
-            for i in (1, 2, 0):
-                wait(ry.at[h, i], ysem.at[h, i])
-            drv[h] = drv[h] - (ry[h, 0] + (ry[h, 1] + ry[h, 2]))
-
-    @at(1.0)
+    tab = {}
+
+    @at(2.0)
     def _():
         wait(owner_s, lsem.at[0])
         wait(pairs_s, lsem.at[1])
@@ -276,78 +248,120 @@
         for t in range(TILES):
             s = jnp.clip(pairs_s[1, t], 0, CL - 1)
             zi = jnp.minimum(lax.rem(lax.shift_right_logical(s, 3) - col + 2 * NX * NZ + 1, NX * NZ), 2)
-            codes[core, t] = jnp.where(t < counts_s[0], zi * (2 * NY) + owner_s[s], -1)
+            codes[row, t] = jnp.where(t < counts_s[0], zi * (2 * NY) + owner_s[s], -1)
         for t in range(TILES, 16):
-            codes[core, t] = -1
-        send(codes.at[core], codes.at[core], bsend.at[2], bsem.at[2], mate, col)
-
-    def weights(dy, t0):
+            codes[row, t] = -1
+        wait(inc, lsem.at[3])
+        for h in range(HALVES):
+            ict[pl.ds(h * NY, NY)] = inc[0, :, h * W:(h + 1) * W].T.reshape(NY, CW, CL)
+        icd[row] = ict[part]
+        wait(tl.at[row], lsem.at[4])
+
+    def exchange(t0):
         @at(t0)
         def _():
-            if dy == 0:
-                wait(codes.at[other], bsem.at[2])
-                wait(tl.at[core], lsem.at[4])
-                wait(tl.at[other], bsem.at[1])
-            for k in range(2):
-                c = [codes[k, t] for t in range(TILES)]
-                for zi in range(3):
-                    for q in range(2):
-                        want = zi * (2 * NY) + at_row(dy) - core + q
-                        found = jnp.int32(-1)
-                        for t in range(TILES):
-                            found = jnp.where(c[t] == want, t, found)
-                        tile = tl[k, jnp.maximum(found, 0)]
-                        wt[dy, pl.ds((k * 2 + q) * CL, CL), pl.ds(zi * CL, CL)] = jnp.where(
-                            found >= 0, tile, jnp.zeros((), BF16))
-
-    for dy in range(NY):
-        weights(dy, 4.0 + 0.9 * dy)
-
-    def sweep(h, s, t0, t1):
-        g = gat[h][s]
-        ys = [lax.rem(y + dy, NY) for dy in range(NY)]
-
+            for i, dy in enumerate((1, 3, 2)):
+                r = peer(dy, 0)[0]
+                wait(tl.at[r], tsem.at[i])
+                send(tl.at[r], tl.at[r], tsend, tsem.at[4 + i], y * 2 + other, col)
+            for i, (dy, flip) in enumerate(peers):
+                r, p = peer(dy, flip)
+                send(ict.at[p], icd.at[row], isend, isem.at[i], r, col)
+                send(codes.at[row], codes.at[row], csend.at[i], csem.at[i], r, col)
+
+    def back(dy):
+        return (NY - dy) % NY
+
+    def summed(t0, t1, t2):
         @at(t0)
         def _():
-            cur = drv[h] if s == 0 else den[h]
-            g[y, 1] = cur.astype(BF16)
-            src = g.at[y, 1]
-            for i in (2, 1, 3, 0):
-                for dc, zi in ((1, 0), (-1, 2), (0, 1)):
-                    if i or dc:
-                        send(src, g.at[y, zi], ssend.at[h, s], ssem.at[h, s, i], at_row(-i), near_col(dc))
+            pos = [position(jnp.int32(r)) for r in range(2 * NY)]
+            for r in range(2 * NY):
+                sp[r] = acc[other, pos[r]].T
+                send(sp.at[r], rp.at[r], psend, psem.at[r], y * 2 + other, col)
+            for r in range(2 * NY):
+                mine[r] = acc[core, pos[r]].T
 
         @at(t1)
         def _():
-            near = None
-            for i in (0, 1, 3, 2):
-                if i:
-                    wait(g.at[ys[i]], ssem.at[h, s, i])
+            for g in range(2):
+                for r in range(g * NY, g * NY + NY):
+                    wait(rp.at[r], psem.at[r])
+                    ts[r] = mine[r] + rp[r]
+                for i, dy in enumerate((2, 1, 3)):
+                    y2 = lax.rem(y + dy, NY)
+                    send(ts.at[pl.ds(g * NY, NY), pl.ds(pl.multiple_of(y2 * CW, CW), CW)],
+                         ry.at[i, pl.ds(g * NY, NY)], ysend, ysem.at[i, g], y2 * 2 + core, col)
+            for i in range(7):
+                dy, flip = peers[i]
+                wait(icd.at[peer(back(dy), flip)[0]], isem.at[i])
+            drv[...] = icd[...] - ts[:, pl.ds(pl.multiple_of(y * CW, CW), CW)]
+
+        @at(t2)
+        def _():
+            for i in (1, 2, 0):
+                for g in range(2):
+                    wait(ry.at[i, pl.ds(g * NY, NY)], ysem.at[i, g])
+            drv[...] = drv[...] - (ry[0] + (ry[1] + ry[2]))
+
+    def sweep(s, t0, t1):
+        g = gat[s]
+
+        @at(t0)
+        def _():
+            if s == 0:
+                for i, (dy, flip) in enumerate(peers):
+                    wait(codes.at[peer(back(dy), flip)[0]], csem.at[i])
+                for i, dy in enumerate((1, 3, 2)):
+                    wait(tl.at[peer(dy, 1)[0]], tsem.at[4 + i])
+                wait(tl.at[peer(0, 1)[0]], tsem.at[3])
+            cur = drv[...] if s == 0 else den[...]
+            g[1] = cur.astype(BF16)
+            send(g.at[1], g.at[0], ssend.at[s], ssem.at[s, 0], row, near_col(1))
+            send(g.at[1], g.at[2], ssend.at[s], ssem.at[s, 1], row, near_col(-1))
+
+        @at(t1)
+        def _():
+            wait(g.at[0], ssem.at[s, 0])
+            wait(g.at[2], ssem.at[s, 1])
+            for r in range(2 * NY):
+                blocks = []
+                for t in range(TILES):
+                    c = codes[r, t]
+                    i = jnp.clip(c, 0, 6 * NY - 1)
+                    u = g[lax.shift_right_logical(i, 3), lax.rem(i, 2 * NY)]
+                    blocks.append(jnp.where(c >= 0, u, jnp.zeros((), BF16)))
+                near = lax.dot_general(
+                    jnp.concatenate(blocks, axis=1), jnp.concatenate([tl[r, t] for t in range(TILES)], axis=1),
+                    (((1,), (1,)), ((), ())), preferred_element_type=F32)
+                d = drv[r]
+                cur = d if s == 0 else den[r]
+                new = cur + DAMPING * (d - cur - near)
+                if s < SWEEPS - 1:
+                    den[r] = new
                 else:
-                    wait(g.at[y, pl.ds(0, 2)], ssem.at[h, s, 0])
-                part = jnp.dot(wt[i], g[ys[i]].reshape(3 * CL, W), preferred_element_type=F32)
-                near = part if near is None else near + part
-            n00, n01, n10, n11 = (near[q * CL:(q + 1) * CL] for q in range(4))
-            near = jnp.where(low, n00 + pltpu.roll(n01, W // 2, 1), pltpu.roll(n10, W // 2, 1) + n11)
-            d = drv[h]
-            cur = d if s == 0 else den[h]
-            new = cur + DAMPING * (d - cur - near)
-            if s < SWEEPS - 1:
-                den[h] = new
-            else:
-                fin[h] = new
-                send(fin.at[h], last.at[h], fsend.at[h], fsem.at[h], mate, col)
-
-    def finish(h, t0):
+                    fin[r] = new
+            if s == SWEEPS - 1:
+                for i, (dy, flip) in enumerate(peers):
+                    r = peer(dy, flip)[0]
+                    send(fin.at[r], last.at[part], fsend, fsem.at[i], r, col)
+                last[part] = fin[row]
+
+    def finish(t0):
         @at(t0)
         def _():
-            wait(last.at[h], fsem.at[h])
-            mine_, theirs = fin[h], pltpu.roll(last[h], W // 2, 1)
-            den[h] = jnp.where(
-                core == 0, jnp.where(low, mine_, theirs), jnp.where(low, theirs, mine_))
-            pltpu.make_async_copy(den.at[h], out.at[0, :, pl.ds(h * W, W)], osem.at[h]).start()
+            for i, (dy, flip) in enumerate(peers):
+                wait(last.at[peer(back(dy), flip)[1]], fsem.at[i])
+            for h in range(HALVES):
+                res[0, :, h * W:(h + 1) * W] = last[pl.ds(h * NY, NY)].reshape(W, CL).T
+            pltpu.make_async_copy(res, out, osem).start()
 
     def loads():
+        pltpu.make_async_copy(incident, inc, lsem.at[3]).start()
+        pltpu.make_async_copy(tiles, tl.at[row], lsem.at[4]).start()
+        for i, dy in enumerate((1, 3, 2)):
+            send(tiles, tl.at[row], tsend, tsem.at[i], peer(back(dy), 0)[0], col)
+        send(tiles, tl.at[row], tsend, tsem.at[3], y * 2 + other, col)
         for a, rel in order:
             gx = lax.rem(x + rel, NX)
             for l in range(LH):
@@ -356,40 +370,33 @@
                     kb.at[a * NX + rel, :, pl.ds(l * NZ * SRC, NZ * SRC)],
                     ksem.at[a * NX + rel, l],
                 ).start()
-        pltpu.make_async_copy(incident, inc.at[core], lsem.at[3]).start()
-        pltpu.make_async_copy(tiles, tl.at[core], lsem.at[4]).start()
-        send(incident, inc.at[core], bsend.at[0], bsem.at[0], mate, col)
-        send(tiles, tl.at[core], bsend.at[1], bsem.at[1], mate, col)
 
     events.append((0.02, 1000, loads))
 
     gather(0, 0.0, 3.2)
     gather(1, 0.01, 3.2)
-    summed(0, 30.0, 31.4, 36.5)
-    summed(1, 30.1, 31.5, 38.5)
-    ST0 = (36.6, 44.0, 51.5, 59.0)
-    ST1 = (38.6, 46.0, 53.5, 61.0)
+    exchange(15.0)
+    summed(30.0, 31.4, 38.0)
     for s in range(SWEEPS):
-        sweep(0, s, ST0[s], ST0[s + 1] - 0.05)
-        sweep(1, s, ST1[s], ST1[s + 1] - 0.05)
-    finish(0, 60.0)
-    finish(1, 62.0)
+        sweep(s, 40.0 + 7 * s, 46.0 + 7 * s)
+    finish(65.0)
 
     for _, _, f in sorted(events, key=lambda e: e[:2]):
         f()
 
-    wait(inc.at[core], bsend.at[0])
-    wait(tl.at[core], bsend.at[1])
-    wait(codes.at[core], bsend.at[2])
+    wait(tl.at[pl.ds(0, 7)], tsend)
+    wait(icd.at[pl.ds(0, 7)], isend)
+    for i in range(7):
+        wait(codes.at[0], csend.at[i])
     for h in range(HALVES):
         for d in range(2):
             wait(hb.at[h, :, pl.ds(0, 3), :, pl.ds(0, 240), :], gsend.at[h, d])
-        wait(sp.at[h], psend.at[h])
-        wait(ts.at[h], ysend.at[h])
-        for s in range(SWEEPS):
-            wait(tl.at[0, pl.ds(0, NY * 3 - 1)], ssend.at[h, s])
-        wait(fin.at[h], fsend.at[h])
-        wait(den.at[h], osem.at[h])
+    wait(sp, psend)
+    wait(ts.at[pl.ds(0, 6)], ysend)
+    for s in range(SWEEPS):
+        wait(gat[s].at[pl.ds(0, 2)], ssend.at[s])
+    wait(fin.at[pl.ds(0, 7)], fsend)
+    wait(res, osem)
 
 
 def per_device(kernels, history, incident, owner, pairs, tiles, counts):
@@ -404,20 +411,20 @@
             pltpu.VMEM((HALVES, 2, NX, LH, NZ * SRC, W), BF16),
             pltpu.VMEM((2 * NX, 8 * CL, DEPTH), BF16),
             pltpu.VMEM((HALVES, 8, CL, W), F32),
-            *[pltpu.VMEM((HALVES, 4, CL, W), F32)] * 3,
-            *[pltpu.VMEM((HALVES, 3, CL, W), F32)] * 2,
-            pltpu.VMEM((2, 1, CL, COLS), F32),
-            *[pltpu.VMEM((HALVES, CL, W), F32)] * 4,
-            pltpu.VMEM((2, TILES, CL, CL), BF16),
-            pltpu.VMEM((NY, 4 * CL, 3 * CL), BF16),
-            *[pltpu.VMEM((NY, 3, CL, W), BF16)] * (HALVES * SWEEPS),
+            *[pltpu.VMEM((8, W, CL), F32)] * 4,
+            pltpu.VMEM((3, 8, CW, CL), F32),
+            pltpu.VMEM((1, CL, COLS), F32),
+            *[pltpu.VMEM((8, CW, CL), F32)] * 6,
+            pltpu.VMEM((1, CL, COLS), F32),
+            pltpu.VMEM((8, TILES, CL, CL), BF16),
+            *[pltpu.VMEM((3, 8, CW, CL), BF16)] * SWEEPS,
             pltpu.SMEM((128,), jnp.int32),
             pltpu.SMEM((2, TILES), jnp.int32),
             pltpu.SMEM((1,), jnp.int32),
-            pltpu.SMEM((2, 16), jnp.int32),
+            pltpu.SMEM((8, 16), jnp.int32),
             dma((5,)), dma((8, LH)), dma((HALVES, 2)), dma((HALVES, 2, 5, 4)), dma((HALVES, 2)),
-            dma((3,)), dma((3,)), dma((HALVES, 4)), dma((HALVES,)), dma((HALVES, 3)), dma((HALVES,)),
-            dma((HALVES, SWEEPS, 4)), dma((HALVES, SWEEPS)), dma((HALVES,)), dma((HALVES,)), dma((HALVES,)),
+            dma((7,)), dma, dma((7,)), dma, dma((7,)), dma((7,)),
+            dma((8,)), dma, dma((3, 2)), dma, dma((SWEEPS, 2)), dma((SWEEPS,)), dma((7,)), dma, dma,
         ],
         compiler_params=pltpu.CompilerParams(
             collective_id=0, has_side_effects=True, vmem_limit_bytes=56 * 2**20

time: 80.9 us -> 76 us (0.939)
  Pallas kernels: 78.6 us -> 73.7 us
    pallas_call x1, Pallas kernels: 78.6 us -> 73.7 us  [per_device(): pl.pallas_call(body, out_shape=jax.ShapeDtypeStruct(incident.shape, F32),...]
where the time goes in v3:
time: 76 us; the launch traced here: 75.9 us
  Pallas kernels  73.7 us (97%)
  local copies, waits for them, and re-layouts  1.57 us (2%)
    pallas_call x1, Pallas kernels, per_device(): pl.pallas_call(body, out_shape=jax.ShapeDtypeStruct(incident.shape, F32),...  73.7 us
    unnamed x1, local copies, waits for them, and re-layouts  1.57 us

profile of v3, /device:TPU:1, one launch (start us, length us, event | category | flops | bytes accessed | tf_op | source)
XLA Modules:
  0.0 75.9 jit_solution(5430863405115485091)
XLA Ops:
  0.7 73.7 %shard_map.73 = f32[1,128,256]{2,1,0:T(8,128)} custom-call(bf16[6,1024,1536]{2,1,0:T(8,128)(2,1)} %kernels.1, bf16[6,96,256]{2,1,0:T(8,128)(2,1)} %history.1, f32[1,128,256]{2,1,0:T(8,128)} %incident.1, s32[128]{0:T(128)} %owner.1, s32[2,12]{1,0:T(2,128)} %bitcast.1, bf16[12,128,128]{2,1,0:T(8,128)(2,1)} %tiles.1, s32[1]{0:T(128)S(6)} %copy.9.counts), custom_call_target="tpu_custom_call" | custom-call | flops 5200000000 | bytes 21000000 | tf_op jit(solution)/shard_map/pallas_call | solution.py:405
  74.3 1.6 %copy.10 = f32[1,128,256]{2,1,0:T(8,128)} copy(f32[1,128,256]{2,1,0:T(8,128)} %shard_map.73) | data formatting | bytes 262144

commit v4 on v3

--- a/solution.py
+++ b/solution.py
@@ -24,7 +24,7 @@
 
 
 def body(kernels, history, incident, owner, pairs, tiles, counts, out,
-         hb, kb, acc, mine, sp, rp, ts, ry, inc, ict, icd, drv, den, fin, last, res, tl,
+         hb, kb, acc, mine, sp, rp, ts, ry, inc, ict, icd, drv, den, fin, last, res, tin, tl,
          gat0, gat1, gat2, owner_s, pairs_s, counts_s, codes,
          lsem, ksem, hsem, gsem, gsend, tsem, tsend, isem, isend, csem, csend,
          psem, psend, ysem, ysend, ssem, ssend, fsem, fsend, osem):
@@ -56,6 +56,7 @@
     barrier = pltpu.get_barrier_semaphore()
     greet = [(row, at_col(1, 0)), (row, at_col(-1, 0)), (row, at_col(0, 1)), (row, at_col(0, -1))]
     greet += [(at_row(1), col), (at_row(-1), col), (at_row(2), col), (y * 2 + other, col)]
+    greet += [(at_row(dy) + other - core, col) for dy in (1, 2, 3)]
     for r, c in greet:
         pl.semaphore_signal(barrier, inc=1, device_id={"row": r, "col": c}, device_id_type=MESH)
 
@@ -239,6 +240,15 @@
         return jnp.minimum(p, NY * 2 - 1)
 
     tab = {}
+
+    @at(1.0)
+    def _():
+        wait(tin, lsem.at[4])
+        for t in range(TILES):
+            tl[row, t] = tin[t].T
+        for i, dy in enumerate((1, 3, 2)):
+            send(tl.at[row], tl.at[row], tsend, tsem.at[i], peer(back(dy), 0)[0], col)
+        send(tl.at[row], tl.at[row], tsend, tsem.at[3], y * 2 + other, col)
 
     @at(2.0)
     def _():
@@ -255,7 +265,10 @@
         for h in range(HALVES):
             ict[pl.ds(h * NY, NY)] = inc[0, :, h * W:(h + 1) * W].T.reshape(NY, CW, CL)
         icd[row] = ict[part]
-        wait(tl.at[row], lsem.at[4])
+        for i, (dy, flip) in enumerate(peers):
+            r, p = peer(dy, flip)
+            send(ict.at[p], icd.at[row], isend, isem.at[i], r, col)
+            send(codes.at[row], codes.at[row], csend.at[i], csem.at[i], r, col)
 
     def exchange(t0):
         @at(t0)
@@ -264,10 +277,6 @@
                 r = peer(dy, 0)[0]
                 wait(tl.at[r], tsem.at[i])
                 send(tl.at[r], tl.at[r], tsend, tsem.at[4 + i], y * 2 + other, col)
-            for i, (dy, flip) in enumerate(peers):
-                r, p = peer(dy, flip)
-                send(ict.at[p], icd.at[row], isend, isem.at[i], r, col)
-                send(codes.at[row], codes.at[row], csend.at[i], csem.at[i], r, col)
 
     def back(dy):
         return (NY - dy) % NY
@@ -299,15 +308,35 @@
 
         @at(t2)
         def _():
-            for i in (1, 2, 0):
-                for g in range(2):
-                    wait(ry.at[i, pl.ds(g * NY, NY)], ysem.at[i, g])
-            drv[...] = drv[...] - (ry[0] + (ry[1] + ry[2]))
-
-    def sweep(s, t0, t1):
+            for g in range(2):
+                rows = pl.ds(g * NY, NY)
+                for i in (1, 2, 0):
+                    wait(ry.at[i, rows], ysem.at[i, g])
+                drv[rows] = drv[rows] - (ry[0, rows] + (ry[1, rows] + ry[2, rows]))
+                gat[0][1, rows] = drv[rows].astype(BF16)
+                halo(0, g)
+
+    def halo(s, g):
+        src = gat[s].at[1, pl.ds(g * NY, NY)]
+        for i, (dc, zi) in enumerate(((1, 0), (-1, 2))):
+            send(src, gat[s].at[zi, pl.ds(g * NY, NY)], ssend.at[s], ssem.at[s, i, g], row, near_col(dc))
+
+    def sweep(s, t1):
         g = gat[s]
 
-        @at(t0)
+        def one(r):
+            blocks = []
+            for t in range(TILES):
+                c = codes[r, t]
+                i = jnp.clip(c, 0, 6 * NY - 1)
+                u = g[lax.shift_right_logical(i, 3), lax.rem(i, 2 * NY)]
+                blocks.append(jnp.where(c >= 0, u, jnp.zeros((), BF16)))
+            near = jnp.dot(jnp.concatenate(blocks, axis=1), tl[r].reshape(TILES * CL, CL), preferred_element_type=F32)
+            d = drv[r]
+            cur = d if s == 0 else den[r]
+            return cur + DAMPING * (d - cur - near)
+
+        @at(t1)
         def _():
             if s == 0:
                 for i, (dy, flip) in enumerate(peers):
@@ -315,37 +344,22 @@
                 for i, dy in enumerate((1, 3, 2)):
                     wait(tl.at[peer(dy, 1)[0]], tsem.at[4 + i])
                 wait(tl.at[peer(0, 1)[0]], tsem.at[3])
-            cur = drv[...] if s == 0 else den[...]
-            g[1] = cur.astype(BF16)
-            send(g.at[1], g.at[0], ssend.at[s], ssem.at[s, 0], row, near_col(1))
-            send(g.at[1], g.at[2], ssend.at[s], ssem.at[s, 1], row, near_col(-1))
-
-        @at(t1)
-        def _():
-            wait(g.at[0], ssem.at[s, 0])
-            wait(g.at[2], ssem.at[s, 1])
-            for r in range(2 * NY):
-                blocks = []
-                for t in range(TILES):
-                    c = codes[r, t]
-                    i = jnp.clip(c, 0, 6 * NY - 1)
-                    u = g[lax.shift_right_logical(i, 3), lax.rem(i, 2 * NY)]
-                    blocks.append(jnp.where(c >= 0, u, jnp.zeros((), BF16)))
-                near = lax.dot_general(
-                    jnp.concatenate(blocks, axis=1), jnp.concatenate([tl[r, t] for t in range(TILES)], axis=1),
-                    (((1,), (1,)), ((), ())), preferred_element_type=F32)
-                d = drv[r]
-                cur = d if s == 0 else den[r]
-                new = cur + DAMPING * (d - cur - near)
-                if s < SWEEPS - 1:
+            for k in range(2):
+                for i, zi in enumerate((0, 2)):
+                    wait(g.at[zi, pl.ds(k * NY, NY)], ssem.at[s, i, k])
+            if s < SWEEPS - 1:
+                for r in range(2 * NY):
+                    new = one(r)
                     den[r] = new
-                else:
-                    fin[r] = new
-            if s == SWEEPS - 1:
+                    gat[s + 1][1, r] = new.astype(BF16)
+                    if r % NY == NY - 1:
+                        halo(s + 1, r // NY)
+            else:
                 for i, (dy, flip) in enumerate(peers):
                     r = peer(dy, flip)[0]
+                    fin[r] = one(r)
                     send(fin.at[r], last.at[part], fsend, fsem.at[i], r, col)
-                last[part] = fin[row]
+                last[part] = one(row)
 
     def finish(t0):
         @at(t0)
@@ -358,10 +372,7 @@
 
     def loads():
         pltpu.make_async_copy(incident, inc, lsem.at[3]).start()
-        pltpu.make_async_copy(tiles, tl.at[row], lsem.at[4]).start()
-        for i, dy in enumerate((1, 3, 2)):
-            send(tiles, tl.at[row], tsend, tsem.at[i], peer(back(dy), 0)[0], col)
-        send(tiles, tl.at[row], tsend, tsem.at[3], y * 2 + other, col)
+        pltpu.make_async_copy(tiles, tin, lsem.at[4]).start()
         for a, rel in order:
             gx = lax.rem(x + rel, NX)
             for l in range(LH):
@@ -375,10 +386,10 @@
 
     gather(0, 0.0, 3.2)
     gather(1, 0.01, 3.2)
-    exchange(15.0)
+    exchange(24.9)
     summed(30.0, 31.4, 38.0)
     for s in range(SWEEPS):
-        sweep(s, 40.0 + 7 * s, 46.0 + 7 * s)
+        sweep(s, 46.0 + 7 * s)
     finish(65.0)
 
     for _, _, f in sorted(events, key=lambda e: e[:2]):
@@ -416,6 +427,7 @@
             pltpu.VMEM((1, CL, COLS), F32),
             *[pltpu.VMEM((8, CW, CL), F32)] * 6,
             pltpu.VMEM((1, CL, COLS), F32),
+            pltpu.VMEM((TILES, CL, CL), BF16),
             pltpu.VMEM((8, TILES, CL, CL), BF16),
             *[pltpu.VMEM((3, 8, CW, CL), BF16)] * SWEEPS,
             pltpu.SMEM((128,), jnp.int32),
@@ -424,7 +436,7 @@
             pltpu.SMEM((8, 16), jnp.int32),
             dma((5,)), dma((8, LH)), dma((HALVES, 2)), dma((HALVES, 2, 5, 4)), dma((HALVES, 2)),
             dma((7,)), dma, dma((7,)), dma, dma((7,)), dma((7,)),
-            dma((8,)), dma, dma((3, 2)), dma, dma((SWEEPS, 2)), dma((SWEEPS,)), dma((7,)), dma, dma,
+            dma((8,)), dma, dma((3, 2)), dma, dma((SWEEPS, 2, 2)), dma((SWEEPS,)), dma((7,)), dma, dma,
         ],
         compiler_params=pltpu.CompilerParams(
             collective_id=0, has_side_effects=True, vmem_limit_bytes=56 * 2**20

time: 76 us -> 72.8 us (0.958)
  Pallas kernels: 73.7 us -> 70.5 us
    pallas_call x1, Pallas kernels: 73.7 us -> 70.5 us  [per_device(): pl.pallas_call(body, out_shape=jax.ShapeDtypeStruct(incident.shape, F32),...]
where the time goes in v4:
time: 72.8 us; the launch traced here: 72.7 us
  Pallas kernels  70.5 us (97%)
  local copies, waits for them, and re-layouts  1.57 us (2%)
    pallas_call x1, Pallas kernels, per_device(): pl.pallas_call(body, out_shape=jax.ShapeDtypeStruct(incident.shape, F32),...  70.5 us
    unnamed x1, local copies, waits for them, and re-layouts  1.57 us

profile of v4, /device:TPU:1, one launch (start us, length us, event | category | flops | bytes accessed | tf_op | source)
XLA Modules:
  0.0 72.7 jit_solution(1011325145231534967)
XLA Ops:
  0.7 70.5 %shard_map.73 = f32[1,128,256]{2,1,0:T(8,128)} custom-call(bf16[6,1024,1536]{2,1,0:T(8,128)(2,1)} %kernels.1, bf16[6,96,256]{2,1,0:T(8,128)(2,1)} %history.1, f32[1,128,256]{2,1,0:T(8,128)} %incident.1, s32[128]{0:T(128)} %owner.1, s32[2,12]{1,0:T(2,128)} %bitcast.1, bf16[12,128,128]{2,1,0:T(8,128)(2,1)} %tiles.1, s32[1]{0:T(128)S(6)} %copy.9.counts), custom_call_target="tpu_custom_call" | custom-call | flops 5200000000 | bytes 21000000 | tf_op jit(solution)/shard_map/pallas_call | solution.py:416
  71.1 1.6 %copy.10 = f32[1,128,256]{2,1,0:T(8,128)} copy(f32[1,128,256]{2,1,0:T(8,128)} %shard_map.73) | data formatting | bytes 262144

commit v5 on v4

--- a/solution.py
+++ b/solution.py
@@ -70,6 +70,7 @@
     for h in range(HALVES):
         for a in range(2):
             pltpu.make_async_copy(own(h, a), piece(h, a, 0, 0), hsem.at[h, a]).start()
+    pltpu.make_async_copy(tiles, tin, lsem.at[4]).start()
     pltpu.make_async_copy(owner, owner_s, lsem.at[0]).start()
     pltpu.make_async_copy(pairs, pairs_s, lsem.at[1]).start()
     pltpu.make_async_copy(counts, counts_s, lsem.at[2]).start()
@@ -241,7 +242,7 @@
 
     tab = {}
 
-    @at(1.0)
+    @at(0.015)
     def _():
         wait(tin, lsem.at[4])
         for t in range(TILES):
@@ -372,7 +373,6 @@
 
     def loads():
         pltpu.make_async_copy(incident, inc, lsem.at[3]).start()
-        pltpu.make_async_copy(tiles, tin, lsem.at[4]).start()
         for a, rel in order:
             gx = lax.rem(x + rel, NX)
             for l in range(LH):

time: 72.8 us -> 72.6 us (level)
  no operation moved by 1% of the time
where the time goes in v5:
time: 72.6 us; the launch traced here: 72.5 us
  Pallas kernels  70.2 us (97%)
  local copies, waits for them, and re-layouts  1.57 us (2%)
    pallas_call x1, Pallas kernels, per_device(): pl.pallas_call(body, out_shape=jax.ShapeDtypeStruct(incident.shape, F32),...  70.2 us
    unnamed x1, local copies, waits for them, and re-layouts  1.57 us

profile of v5, /device:TPU:1, one launch (start us, length us, event | category | flops | bytes accessed | tf_op | source)
XLA Modules:
  0.0 72.5 jit_solution(6358893377953038284)
XLA Ops:
  0.7 70.2 %shard_map.73 = f32[1,128,256]{2,1,0:T(8,128)} custom-call(bf16[6,1024,1536]{2,1,0:T(8,128)(2,1)} %kernels.1, bf16[6,96,256]{2,1,0:T(8,128)(2,1)} %history.1, f32[1,128,256]{2,1,0:T(8,128)} %incident.1, s32[128]{0:T(128)} %owner.1, s32[2,12]{1,0:T(2,128)} %bitcast.1, bf16[12,128,128]{2,1,0:T(8,128)(2,1)} %tiles.1, s32[1]{0:T(128)S(6)} %copy.9.counts), custom_call_target="tpu_custom_call" | custom-call | flops 5200000000 | bytes 21000000 | tf_op jit(solution)/shard_map/pallas_call | solution.py:416
  70.9 1.6 %copy.10 = f32[1,128,256]{2,1,0:T(8,128)} copy(f32[1,128,256]{2,1,0:T(8,128)} %shard_map.73) | data formatting | bytes 262144

commit v6 on v4

--- a/solution.py
+++ b/solution.py
@@ -293,14 +293,14 @@
 
         @at(t1)
         def _():
-            for g in range(2):
-                for r in range(g * NY, g * NY + NY):
+            for g in range(NY):
+                for r in range(g * 2, g * 2 + 2):
                     wait(rp.at[r], psem.at[r])
                     ts[r] = mine[r] + rp[r]
                 for i, dy in enumerate((2, 1, 3)):
                     y2 = lax.rem(y + dy, NY)
-                    send(ts.at[pl.ds(g * NY, NY), pl.ds(pl.multiple_of(y2 * CW, CW), CW)],
-                         ry.at[i, pl.ds(g * NY, NY)], ysend, ysem.at[i, g], y2 * 2 + core, col)
+                    send(ts.at[pl.ds(g * 2, 2), pl.ds(pl.multiple_of(y2 * CW, CW), CW)],
+                         ry.at[i, pl.ds(g * 2, 2)], ysend, ysem.at[i, g], y2 * 2 + core, col)
             for i in range(7):
                 dy, flip = peers[i]
                 wait(icd.at[peer(back(dy), flip)[0]], isem.at[i])
@@ -311,7 +311,8 @@
             for g in range(2):
                 rows = pl.ds(g * NY, NY)
                 for i in (1, 2, 0):
-                    wait(ry.at[i, rows], ysem.at[i, g])
+                    for q in (2 * g, 2 * g + 1):
+                        wait(ry.at[i, pl.ds(q * 2, 2)], ysem.at[i, q])
                 drv[rows] = drv[rows] - (ry[0, rows] + (ry[1, rows] + ry[2, rows]))
                 gat[0][1, rows] = drv[rows].astype(BF16)
                 halo(0, g)
@@ -436,7 +437,7 @@
             pltpu.SMEM((8, 16), jnp.int32),
             dma((5,)), dma((8, LH)), dma((HALVES, 2)), dma((HALVES, 2, 5, 4)), dma((HALVES, 2)),
             dma((7,)), dma, dma((7,)), dma, dma((7,)), dma((7,)),
-            dma((8,)), dma, dma((3, 2)), dma, dma((SWEEPS, 2, 2)), dma((SWEEPS,)), dma((7,)), dma, dma,
+            dma((8,)), dma, dma((3, NY)), dma, dma((SWEEPS, 2, 2)), dma((SWEEPS,)), dma((7,)), dma, dma,
         ],
         compiler_params=pltpu.CompilerParams(
             collective_id=0, has_side_effects=True, vmem_limit_bytes=56 * 2**20

time: 72.8 us -> 72.7 us (level)
  no operation moved by 1% of the time
where the time goes in v6:
time: 72.7 us; the launch traced here: 72.5 us
  Pallas kernels  70.3 us (97%)
  local copies, waits for them, and re-layouts  1.57 us (2%)
    pallas_call x1, Pallas kernels, per_device(): pl.pallas_call(body, out_shape=jax.ShapeDtypeStruct(incident.shape, F32),...  70.3 us
    unnamed x1, local copies, waits for them, and re-layouts  1.57 us

profile of v6, /device:TPU:1, one launch (start us, length us, event | category | flops | bytes accessed | tf_op | source)
XLA Modules:
  0.0 72.5 jit_solution(912671467989008240)
XLA Ops:
  0.7 70.3 %shard_map.73 = f32[1,128,256]{2,1,0:T(8,128)} custom-call(bf16[6,1024,1536]{2,1,0:T(8,128)(2,1)} %kernels.1, bf16[6,96,256]{2,1,0:T(8,128)(2,1)} %history.1, f32[1,128,256]{2,1,0:T(8,128)} %incident.1, s32[128]{0:T(128)} %owner.1, s32[2,12]{1,0:T(2,128)} %bitcast.1, bf16[12,128,128]{2,1,0:T(8,128)(2,1)} %tiles.1, s32[1]{0:T(128)S(6)} %copy.9.counts), custom_call_target="tpu_custom_call" | custom-call | flops 5200000000 | bytes 21000000 | tf_op jit(solution)/shard_map/pallas_call | solution.py:417
  71.0 1.6 %copy.10 = f32[1,128,256]{2,1,0:T(8,128)} copy(f32[1,128,256]{2,1,0:T(8,128)} %shard_map.73) | data formatting | bytes 262144
